TPU v7x, 32 devices: a whole 2x2x4 slice. The times are simulated.
32 devices in a mesh: half: 2 (over core), dom: 8 (over z, y), slab: 2 (over x).
Axes of the slice: x: 2, y: 2, z: 4, core: 2. Of those that a mesh axis runs over, the one named last changes fastest.
Arguments:
- volume: float32 [2, 2048, 400], P('half', 'slab')
- images: bfloat16 [2, 8192, 400], P('half', 'dom'), may hold values from -18 to 18
- tap_index: int32 [2, 2, 8, 8192], P('half', 'slab', None, 'dom'), may hold values from 0 to 1023, as said below
- tap_weight: float32 [2, 2, 8, 8192], P('half', 'slab', None, 'dom'), may hold values from 0.2 to 1
- classes: int32 [2, 128], P('half', 'dom'), may hold values from 0 to 15
- shifts: int32 [2, 2, 128], P('half', None, 'dom'), may hold values from -8 to 8
- defocus: float32 [16], replicated, may hold values from 0.5 to 3
Outputs:
- updated: float32 [2, 2048, 400], P('half', 'slab')
Inputs may be any that keep to these rules, and one draw needn't show every extreme that they name: `tap_index`: the 8 taps of one line and slab read 8 consecutive map lines.
All inputs are finite; a program needn't handle non-finite values.
Results may differ from a plain program's by a relative error of at most 0.0035.
Values may be sent and summed in bfloat16 or wider, within the bound.
A program may use at most 64 MiB of HBM per device.

v0:
```python
import math

import jax
import jax.numpy as jnp
from jax import lax
from jax.sharding import PartitionSpec as P

LPI = 64


CTF_GAIN = 30.0
PHASE_ZERO = 0.1
STEP_SCALE = 0.5


def swapped(value, axis, distance):
    mask = 2**distance
    pairs = [(source, source ^ mask) for source in range(lax.axis_size(axis))]
    return lax.ppermute(value, axis, pairs)


def line_terms(classes_local, shifts_local, defocus, radii):
    radius = jnp.arange(radii, dtype=jnp.float32)
    class_ids = jnp.arange(defocus.shape[0], dtype=jnp.int32)
    focus = jnp.sum(
        jnp.where(classes_local[:, None] == class_ids[None, :], defocus[None, :], 0.0), axis=1
    )
    ctf_part = -jnp.sin(CTF_GAIN * focus[:, None] * (radius[None, :] / radii) ** 2 + PHASE_ZERO)
    ctf_rows = jnp.repeat(ctf_part, LPI, axis=0)
    theta = jnp.pi * jnp.arange(LPI, dtype=jnp.float32) / LPI
    theta_rows = jnp.tile(theta, classes_local.shape[0])
    shift_x = jnp.repeat(shifts_local[0].astype(jnp.float32), LPI)
    shift_y = jnp.repeat(shifts_local[1].astype(jnp.float32), LPI)
    along = shift_x * jnp.cos(theta_rows) + shift_y * jnp.sin(theta_rows)
    phase = 2.0 * jnp.pi * radius[None, :] * along[:, None] / (2.0 * radii)
    return (ctf_rows, jnp.cos(phase), jnp.sin(phase))


def weighted_back(proj, data, ctf_rows, cosine, sine_part, radii):
    proj_re, proj_im = (proj[:, :radii], proj[:, radii:])
    data_f = data.astype(jnp.float32)
    res_re = ctf_rows * (cosine * proj_re - sine_part * proj_im) - data_f[:, :radii]
    res_im = ctf_rows * (sine_part * proj_re + cosine * proj_im) - data_f[:, radii:]
    back_re = ctf_rows * (cosine * res_re + sine_part * res_im)
    back_im = ctf_rows * (cosine * res_im - sine_part * res_re)
    return jnp.concatenate([back_re, back_im], axis=1).astype(jnp.bfloat16)


def shell_terms(mine, other, radii):
    num = jnp.sum(mine[:, :radii] * other[:, :radii] + mine[:, radii:] * other[:, radii:], axis=0)
    den_mine = jnp.sum(mine[:, :radii] ** 2 + mine[:, radii:] ** 2, axis=0)
    den_other = jnp.sum(other[:, :radii] ** 2 + other[:, radii:] ** 2, axis=0)
    return (num, den_mine, den_other)


def shell_factor(totals):
    num, den_mine, den_other = totals
    fsc = num / (jnp.sqrt(den_mine * den_other) + 1e-06)
    return jnp.tile((1.0 + fsc) / 2.0, 2)


def spread_back(taps_at, taps_wide, back_wide, start, count):
    total = jnp.zeros((count, back_wide.shape[1]), jnp.float32)
    for tap_num in range(taps_at.shape[0]):
        local = taps_at[tap_num] - start
        inside = jnp.logical_and(local >= 0, local < count)
        local = jnp.where(inside, local, count)
        total = total.at[local].add(taps_wide[tap_num][:, None] * back_wide, mode="drop")
    return total


def body(volume, images, tap_index, tap_weight, classes, shifts, defocus):
    slab_map = volume[0]
    lines_slab = slab_map.shape[0]
    radii = slab_map.shape[1] // 2
    data = images[0]
    rows = data.shape[0]
    taps_at = tap_index[0, 0]
    taps_wide = tap_weight[0, 0].astype(jnp.bfloat16).astype(jnp.float32)
    map_low = slab_map.astype(jnp.bfloat16)
    partial_value = jnp.zeros((rows, 2 * radii), jnp.float32)
    for tap_num in range(taps_at.shape[0]):
        picked = jnp.take(map_low, taps_at[tap_num], axis=0)
        partial_value = partial_value + taps_wide[tap_num][:, None] * picked.astype(jnp.float32)
    ctf_rows, cosine, sine_part = line_terms(classes[0], shifts[0], defocus, radii)
    share = rows // lax.axis_size("slab")
    begin = lax.axis_index("slab") * share
    proj_share = lax.psum_scatter(partial_value, "slab", scatter_dimension=0, tiled=True)
    back_share = weighted_back(
        proj_share,
        lax.dynamic_slice_in_dim(data, begin, share, 0),
        lax.dynamic_slice_in_dim(ctf_rows, begin, share, 0),
        lax.dynamic_slice_in_dim(cosine, begin, share, 0),
        lax.dynamic_slice_in_dim(sine_part, begin, share, 0),
        radii,
    )
    back = lax.all_gather(back_share, "slab", axis=0, tiled=True)
    back_wide = back.astype(jnp.float32)
    step = STEP_SCALE / math.sqrt(rows * lax.axis_size("dom") * taps_at.shape[0] / lines_slab)
    local_grad = spread_back(taps_at, taps_wide, back_wide, 0, lines_slab)
    grad = lax.psum(local_grad, "dom")
    cand = slab_map - step * grad
    other = swapped(cand.astype(jnp.bfloat16), "half", 0).astype(cand.dtype)
    totals = lax.psum(shell_terms(cand, other, radii), "slab")
    result = slab_map - step * shell_factor(totals)[None, :] * grad
    return result[None]


def solution(mesh):
    placed = (
        P("half", "slab", None),
        P("half", "dom", None),
        P("half", "slab", None, "dom"),
        P("half", "slab", None, "dom"),
        P("half", "dom"),
        P("half", None, "dom"),
        P(),
    )
    return jax.shard_map(
        body, mesh=mesh, in_specs=placed, out_specs=P("half", "slab", None), check_vma=False
    )
```

profile of v0, /device:TPU:0, one launch (start us, length us, event | category | flops | bytes accessed | tf_op | source)
XLA Modules:
  0.0 325.4 jit_solution(9676088225571574368)
XLA Ops:
  12.5 4.0 %gather_fusion.2 = bf16[1024,400]{1,0:T(8,128)(2,1)S(1)} fusion(bf16[1024,400]{1,0:T(8,128)(2,1)S(1)} %bitcast_convert_fusion, s32[1024]{0:T(1024)S(1)} %fusion.20), kind=kCustom, calls=%fused_computation.2.clone | custom fusion | bytes 1642496 | tf_op jit(solution)/shard_map/jit(_take)/gather | solution.py:83
  16.4 5.1 %gather_fusion.3 = bf16[1024,400]{1,0:T(8,128)(2,1)} fusion(bf16[1024,400]{1,0:T(8,128)(2,1)S(1)} %bitcast_convert_fusion, s32[1024]{0:T(1024)S(1)} %fusion.21), kind=kCustom, calls=%fused_computation.3.clone | custom fusion | bytes 1642496 | tf_op jit(solution)/shard_map/jit(_take)/gather | solution.py:83
  21.5 5.1 %gather_fusion.4 = bf16[1024,400]{1,0:T(8,128)(2,1)} fusion(bf16[1024,400]{1,0:T(8,128)(2,1)S(1)} %bitcast_convert_fusion, s32[1024]{0:T(1024)S(1)} %fusion.22), kind=kCustom, calls=%fused_computation.4.clone | custom fusion | bytes 1642496 | tf_op jit(solution)/shard_map/jit(_take)/gather | solution.py:83
  26.6 5.1 %gather_fusion.5 = bf16[1024,400]{1,0:T(8,128)(2,1)} fusion(bf16[1024,400]{1,0:T(8,128)(2,1)S(1)} %bitcast_convert_fusion, s32[1024]{0:T(1024)S(1)} %fusion.23), kind=kCustom, calls=%fused_computation.5.clone | custom fusion | bytes 1642496 | tf_op jit(solution)/shard_map/jit(_take)/gather | solution.py:83
  31.6 5.1 %gather_fusion.6 = bf16[1024,400]{1,0:T(8,128)(2,1)} fusion(bf16[1024,400]{1,0:T(8,128)(2,1)S(1)} %bitcast_convert_fusion, s32[1024]{0:T(1024)S(1)} %fusion.24), kind=kCustom, calls=%fused_computation.6.clone | custom fusion | bytes 1642496 | tf_op jit(solution)/shard_map/jit(_take)/gather | solution.py:83
  36.7 5.1 %gather_fusion.7 = bf16[1024,400]{1,0:T(8,128)(2,1)} fusion(bf16[1024,400]{1,0:T(8,128)(2,1)S(1)} %bitcast_convert_fusion, s32[1024]{0:T(1024)S(1)} %fusion.25), kind=kCustom, calls=%fused_computation.7.clone | custom fusion | bytes 1642496 | tf_op jit(solution)/shard_map/jit(_take)/gather | solution.py:83
  41.8 5.1 %gather_fusion = bf16[1024,400]{1,0:T(8,128)(2,1)} fusion(bf16[1024,400]{1,0:T(8,128)(2,1)S(1)} %bitcast_convert_fusion, s32[1024]{0:T(1024)S(1)} %fusion.18), kind=kCustom, calls=%fused_computation.clone | custom fusion | bytes 1642496 | tf_op jit(solution)/shard_map/jit(_take)/gather | solution.py:83
  46.8 5.1 %gather_fusion.1 = bf16[1024,400]{1,0:T(8,128)(2,1)} fusion(bf16[1024,400]{1,0:T(8,128)(2,1)S(1)} %bitcast_convert_fusion, s32[1024]{0:T(1024)S(1)} %fusion.19), kind=kCustom, calls=%fused_computation.1.clone | custom fusion | bytes 1642496 | tf_op jit(solution)/shard_map/jit(_take)/gather | solution.py:83
  51.9 8.2 %multiply_add_fusion = f32[1024,400]{1,0:T(8,128)} fusion(bf16[1024,400]{1,0:T(8,128)(2,1)} %gather_fusion.7, bf16[1024,400]{1,0:T(8,128)(2,1)} %gather_fusion.6, bf16[1024,400]{1,0:T(8,128)(2,1)} %gather_fusion.5, bf16[1024,400]{1,0:T(8,128)(2,1)} %gather_fusion.4, bf16[1024,400]{1,0:T(8,128)(2,1)} %gather_fusion.3, bf16[1024,400]{1,0:T(8,128)(2,1)S(1)} %gather_fusion.2, ...), kind=kLoop, calls=%fused_computation.36 | loop fusion | flops 12697600 | bytes 8232960 | tf_op jit(solution)/shard_map/add | solution.py:84
  61.8 33.1 %reduce-scatter.2.cloned.1.call-done = f32[512,400]{1,0:T(8,128)} async-done(((f32[1024,400]{1,0:T(8,128)}), f32[512,400]{1,0:T(8,128)}) %reduce-scatter.2.cloned.1.call-update) | async-done | bytes 819216 | tf_op jit(solution)/shard_map/reduce_scatter | solution.py:88
  95.0 3.8 %multiply_convert_fusion.1 = (bf16[512,200]{1,0:T(8,128)(2,1)S(1)}, bf16[512,200]{1,0:T(8,128)(2,1)S(1)}) fusion(f32[512,400]{1,0:T(8,128)S(1)} %bitcast_convert_fusion.1, f32[512,400]{1,0:T(8,128)} %reduce-scatter.2.cloned.1.call-done, f32[1024,200]{1,0:T(8,128)S(1)} %bitcast.58, s32[]{:T(128)S(6)} %select_n.181, f32[1024,200]{1,0:T(8,128)S(1)} %multiply_multiply_fusion), kind=kLoop, calls=%fused_computation.55 | loop fusion | flops 2048000 | bytes 2867204 | tf_op jit(solution)/shard_map/convert.1
  99.0 14.3 %all_gather.3 = bf16[1024,400]{1,0:T(8,128)(2,1)S(1)} all-gather(bf16[512,400]{1,0:T(8,128)(2,1)S(1)} %pad_maximum_fusion), channel_id=1, replica_groups=mesh['half'=2,'dom'=8,'slab'=2] {'slab'}, dimensions={0}, use_global_device_ids=true | all-gather | bytes 1228800 | tf_op jit(solution)/shard_map/all_gather | solution.py:97
  113.3 8.5 %scatter_custom_fusion = f32[1024,400]{1,0:T(8,128)} fusion(s32[1024]{0:T(1024)S(1)} %bitcast.98, bf16[1024,400]{1,0:T(8,128)(2,1)S(1)} %all_gather.3, f32[1024]{0:T(1024)S(1)} %bitcast.74, f32[]{:T(128)} %constant.23.clone.1), kind=kCustom, calls=%fused_computation.24 | custom fusion | flops 1228800 | bytes 2691076 | tf_op jit(solution)/shard_map/scatter-add | solution.py:68
  121.8 10.0 %scatter_custom_fusion.1 = f32[1024,400]{1,0:T(8,128)} fusion(f32[1024,400]{1,0:T(8,128)} %scatter_custom_fusion, s32[1024]{0:T(1024)S(1)} %bitcast.97, bf16[1024,400]{1,0:T(8,128)(2,1)S(1)} %all_gather.3, f32[1024]{0:T(1024)S(1)} %bitcast.72), kind=kCustom, calls=%fused_computation.25 | custom fusion | flops 1228800 | bytes 2691072 | tf_op jit(solution)/shard_map/scatter-add | solution.py:68
  131.8 10.0 %scatter_custom_fusion.2 = f32[1024,400]{1,0:T(8,128)} fusion(f32[1024,400]{1,0:T(8,128)} %scatter_custom_fusion.1, s32[1024]{0:T(1024)S(1)} %bitcast.96, bf16[1024,400]{1,0:T(8,128)(2,1)S(1)} %all_gather.3, f32[1024]{0:T(1024)S(1)} %bitcast.70), kind=kCustom, calls=%fused_computation.26 | custom fusion | flops 1228800 | bytes 2691072 | tf_op jit(solution)/shard_map/scatter-add | solution.py:68
  141.8 10.0 %scatter_custom_fusion.3 = f32[1024,400]{1,0:T(8,128)} fusion(f32[1024,400]{1,0:T(8,128)} %scatter_custom_fusion.2, s32[1024]{0:T(1024)S(1)} %bitcast.95, bf16[1024,400]{1,0:T(8,128)(2,1)S(1)} %all_gather.3, f32[1024]{0:T(1024)S(1)} %bitcast.68), kind=kCustom, calls=%fused_computation.27 | custom fusion | flops 1228800 | bytes 2691072 | tf_op jit(solution)/shard_map/scatter-add | solution.py:68
  151.8 10.0 %scatter_custom_fusion.4 = f32[1024,400]{1,0:T(8,128)} fusion(f32[1024,400]{1,0:T(8,128)} %scatter_custom_fusion.3, s32[1024]{0:T(1024)S(1)} %bitcast.94, bf16[1024,400]{1,0:T(8,128)(2,1)S(1)} %all_gather.3, f32[1024]{0:T(1024)S(1)} %bitcast.66), kind=kCustom, calls=%fused_computation.28 | custom fusion | flops 1228800 | bytes 2691072 | tf_op jit(solution)/shard_map/scatter-add | solution.py:68
  161.8 10.0 %scatter_custom_fusion.5 = f32[1024,400]{1,0:T(8,128)} fusion(f32[1024,400]{1,0:T(8,128)} %scatter_custom_fusion.4, s32[1024]{0:T(1024)S(1)} %bitcast.93, bf16[1024,400]{1,0:T(8,128)(2,1)S(1)} %all_gather.3, f32[1024]{0:T(1024)S(1)} %bitcast.64), kind=kCustom, calls=%fused_computation.29 | custom fusion | flops 1228800 | bytes 2691072 | tf_op jit(solution)/shard_map/scatter-add | solution.py:68
  171.8 10.0 %scatter_custom_fusion.6 = f32[1024,400]{1,0:T(8,128)} fusion(f32[1024,400]{1,0:T(8,128)} %scatter_custom_fusion.5, s32[1024]{0:T(1024)S(1)} %bitcast.92, bf16[1024,400]{1,0:T(8,128)(2,1)S(1)} %all_gather.3, f32[1024]{0:T(1024)S(1)} %bitcast.62), kind=kCustom, calls=%fused_computation.30 | custom fusion | flops 1228800 | bytes 2691072 | tf_op jit(solution)/shard_map/scatter-add | solution.py:68
  181.8 10.0 %scatter_custom_fusion.7 = f32[1024,400]{1,0:T(8,128)} fusion(f32[1024,400]{1,0:T(8,128)} %scatter_custom_fusion.6, s32[1024]{0:T(1024)S(1)} %bitcast.91, bf16[1024,400]{1,0:T(8,128)(2,1)S(1)} %all_gather.3, f32[1024]{0:T(1024)S(1)} %bitcast.60), kind=kCustom, calls=%fused_computation.31 | custom fusion | flops 1228800 | bytes 2691072 | tf_op jit(solution)/shard_map/scatter-add | solution.py:68
  191.8 102.0 %all-reduce.3.cloned.1.call-done = f32[1024,400]{1,0:T(8,128)} async-done(((f32[1024,400]{1,0:T(8,128)}), f32[1024,400]{1,0:T(8,128)}) %all-reduce.3.cloned.1.call-update) | async-done | bytes 1638416 | tf_op jit(solution)/shard_map/psum | solution.py:101
  293.8 3.8 %fusion.28 = (bf16[1024,400]{1,0:T(8,128)(2,1)}, f32[1024,400]{1,0:T(8,128)}) fusion(f32[1024,400]{1,0:T(8,128)} %all-reduce.3.cloned.1.call-done, f32[1,1024,400]{2,1,0:T(8,128)S(1)} %copy-done.1), kind=kLoop, calls=%fused_computation.114 | loop fusion | flops 1228800 | bytes 5734400 | tf_op jit(solution)/shard_map/convert_element_type | solution.py:103
  307.3 4.9 %all-reduce = (f32[200]{0:T(256)S(1)}, f32[200]{0:T(256)S(1)}, f32[200]{0:T(256)S(1)}) all-reduce(f32[200]{0:T(256)S(1)} %get-tuple-element.7, f32[200]{0:T(256)S(1)} %get-tuple-element.8, f32[200]{0:T(256)S(1)} %get-tuple-element.6), channel_id=1, replica_groups=mesh['half'=2,'dom'=8,'slab'=2] {'slab'}, use_global_device_ids=true, to_apply=%region_12.14 | all-reduce | flops 600 | bytes 4800 | tf_op jit(solution)/shard_map/psum | solution.py:104
  312.4 3.5 %fusion.8 = f32[1,1024,400]{2,1,0:T(8,128)} fusion(f32[1,1024,400]{2,1,0:T(8,128)S(1)} %copy-done.1, f32[1024,400]{1,0:T(8,128)} %all-reduce.3.cloned.1.call-done, f32[400]{0:T(512)S(1)} %mul.332), kind=kLoop, calls=%fused_computation.35 | loop fusion | flops 819200 | bytes 4916800 | tf_op jit(solution)/shard_map/broadcast_in_dim | solution.py:106
  (63 shorter events, 20.3 us)
Async XLA Ops:
  6.5 53.7 %copy-start = (bf16[1,1024,400]{1,2,0:T(8,128)(2,1)S(1)}, bf16[1,1024,400]{1,2,0:T(8,128)(2,1)}, u32[]{:S(2)}) copy-start(bf16[1,1024,400]{1,2,0:T(8,128)(2,1)} %param.10) | copy-start | bytes 2457604
  6.5 88.4 %reduce-scatter.2.cloned.1.call-start = ((), (), s32[]{:S(2)}) async-start(), calls=%async_computation.1 | async-start | bytes 3145728 | tf_op jit(solution)/shard_map/reduce_scatter | solution.py:88
  46.8 5.1 %copy-start.4 = (f32[1,1,8,1024]{3,2,1,0:T(8,128)S(1)}, f32[1,1,8,1024]{3,2,1,0:T(8,128)}, u32[]{:S(2)}) copy-start(f32[1,1,8,1024]{3,2,1,0:T(8,128)} %param.12) | copy-start | bytes 98308
  60.1 0.7 copy-start.5
  60.1 0.9 copy-start.6
  60.1 0.9 copy-start.7
  60.1 1.2 copy-start.3
  60.2 233.6 %all-reduce.3.cloned.1.call-start = ((), (), s32[]{:S(2)}) async-start(), calls=%async_computation.2 | async-start | bytes 4194304 | tf_op jit(solution)/shard_map/psum | solution.py:101
  191.8 102.0 %copy-start.1 = (f32[1,1024,400]{2,1,0:T(8,128)S(1)}, f32[1,1024,400]{2,1,0:T(8,128)}, u32[]{:S(2)}) copy-start(f32[1,1024,400]{2,1,0:T(8,128)} %copy.19) | copy-start | bytes 4915204
  299.8 2.7 collective-permute-start
  304.7 1.9 copy-start.2
Sparse Core Ops, SparseCore 0:
  60.3 34.5 reduce-scatter.1
  191.9 101.8 all-reduce.2
where the time goes:
time: 326 us; the launch traced here: 325 us
  waiting for transfers between devices  138 us (42%)
  other arithmetic  103 us (32%)
  local copies, waits for them, and re-layouts  51.7 us (16%)
  blocking collectives  19.3 us (6%)
  between operations  13.7 us (4%)
    psum x1, waiting for transfers between devices, body(): grad = lax.psum(local_grad, 'dom')  102 us
    scatter-add x8, other arithmetic, spread_back(): total.at[local].add(taps_wide[tap_num][:, None] * back_wide, mode='drop')  78.5 us
    gather x8, local copies, waits for them, and re-layouts, body(): picked = jnp.take(map_low, taps_at[tap_num], axis=0)  39.4 us
    reduce_scatter x1, waiting for transfers between devices, body(): lax.psum_scatter(partial_value, 'slab', scatter_dimension=0, tiled=True)  33.1 us
    all_gather x1, blocking collectives, body(): back = lax.all_gather(back_share, 'slab', axis=0, tiled=True)  14.3 us
    add x1, other arithmetic, body(): partial_value + taps_wide[tap_num][:, None] * picked.astype(jnp.float32)  8.19 us
  transfers between devices with their start and end apart: 3, of which 3 were waited for; matrix products, arithmetic and copies ran while one was open for 0% of the time, Pallas kernels for 0%

commit v1 on v0

v1 whole, which is shorter than its diff:
```python
import functools
import math

import jax
import jax.numpy as jnp
from jax import lax
from jax.experimental import pallas as pl
from jax.experimental.pallas import tpu as pltpu
from jax.sharding import PartitionSpec as P

LPI = 64
CTF_GAIN = 30.0
PHASE_ZERO = 0.1
STEP_SCALE = 0.5
CHUNK = 128
MESH = pl.DeviceIdType.MESH
F32 = jnp.float32
BF16 = jnp.bfloat16


def sine(x):
    turns = jnp.floor(x * (1.0 / math.pi) + 0.5)
    y = ((x - turns * 3.140625) - turns * 9.67502593994140625e-4) - turns * 1.509957990978376432e-7
    odd = turns - 2.0 * jnp.floor(turns * 0.5)
    y2 = y * y
    poly = -1.0 / 39916800.0
    for inverse in (1.0 / 362880.0, -1.0 / 5040.0, 1.0 / 120.0, -1.0 / 6.0, 1.0):
        poly = poly * y2 + inverse
    return (y * poly) * (1.0 - 2.0 * odd)


def mul_nt(a, b, precision=None):
    return lax.dot_general(
        a, b, (((1,), (1,)), ((), ())), preferred_element_type=F32, precision=precision
    )


def eye(n, kind):
    row = lax.broadcasted_iota(jnp.int32, (n, n), 0)
    col = lax.broadcasted_iota(jnp.int32, (n, n), 1)
    return jnp.where(row == col, 1.0, 0.0).astype(kind)


def remote(src, dst, send, recv, where):
    return pltpu.make_async_remote_copy(
        src_ref=src, dst_ref=dst, send_sem=send, recv_sem=recv, device_id=where, device_id_type=MESH
    )


def build_matrix(taps_ref, wide_ref):
    packed = taps_ref[...].astype(F32)
    value = jnp.concatenate([packed[:8], packed[:8]], axis=0)
    block = jnp.concatenate([packed[8:], packed[8:] - 1.0], axis=0)

    @pl.loop(0, wide_ref.shape[0] // 32)
    def _(t):
        for u in range(2):
            b = (4 * t + 2 * u).astype(F32)
            rows = pl.ds(pl.multiple_of(t * 32 + 16 * u, 16), 16)
            wide_ref[rows, :] = jnp.where(block == b, value, 0.0).astype(BF16)


def kernel(
    n_dom, n_slab, step,
    vol, img, taps, wts, cls, shf, dfc,
    out,
    mapt, omap, ptap, otap, wide, owide, work, proj, square, back,
    gown, s1send, s1recv, s2send, s2recv, gall, cand, ocand, fs, fx, fy, fz,
    tap_s, tap_r, x_s, x_r, y_s, y_r, p_s, p_r, q_s, q_r, g_s, g_r, f_s, f_r, c_s, c_r,
    ux_s, ux_r, uy_s, uy_r, uz_s, uz_r,
):
    h, d, s = lax.axis_index("half"), lax.axis_index("dom"), lax.axis_index("slab")
    lines, cols = vol.shape
    radii = cols // 2
    rows = img.shape[0]
    nz = n_dom // 2
    y, z = lax.rem(d, 2), d // 2
    pair = (h, d + 1 - 2 * y, s)
    other_half = (1 - h, d, s)
    peers = [(h, d, lax.rem(s + p, n_slab)) for p in range(1, n_slab)]
    zs = [lax.rem(z + 1 + t, nz) for t in range(nz)]
    zpeers = [(h, 2 * zs[t] + y, s) for t in range(nz - 1)]
    bw = lines // n_dom
    nj = lines // CHUNK // 2

    barrier = pltpu.get_barrier_semaphore()
    everyone = [pair, other_half] + peers + zpeers
    for who in everyone:
        pl.semaphore_signal(barrier, inc=1, device_id=who, device_id_type=MESH)

    sub = lax.broadcasted_iota(jnp.int32, (8, rows), 0)
    value = jnp.zeros((8, rows), F32)
    block = jnp.zeros((8, rows), F32)
    for k in range(8):
        line = taps[k:k + 1, :]
        hit = jnp.bitwise_and(line, 7) == sub
        value = jnp.where(hit, wts[k:k + 1, :], value)
        block = jnp.where(hit, lax.shift_right_logical(line, 3).astype(F32), block)
    ptap[...] = jnp.concatenate([value, block], axis=0).astype(BF16)

    ident = eye(cols, BF16)

    def map_chunk(c):
        part = vol[pl.ds(pl.multiple_of(c * CHUNK, CHUNK), CHUNK), :].astype(BF16)
        mapt[c] = mul_nt(ident, part).astype(BF16)

    pl.loop(0, 2 * nj)(map_chunk)

    pl.semaphore_wait(barrier, len(everyone))
    sends = []

    def go(copy):
        copy.start()
        sends.append(copy)
        return copy

    tap_copies = [go(remote(ptap, otap.at[p], tap_s.at[p], tap_r.at[p], peers[p])) for p in range(n_slab - 1)]
    x_copies = [
        [
            go(remote(mapt.at[2 * j + y], omap.at[p, 2 * j + y], x_s.at[p, j], x_r.at[p, j], peers[p]))
            for j in range(nj)
        ]
        for p in range(n_slab - 1)
    ]
    y_copies = [[None] * nj for p in range(n_slab - 1)]

    def forward(j):
        for p in range(n_slab - 1):
            x_copies[p][j].wait_recv()
            slot = omap.at[p, 2 * j + y]
            y_copies[p][j] = go(remote(slot, slot, y_s.at[p, j], y_r.at[p, j], pair))

    build_matrix(ptap, wide)

    @pl.loop(0, rows // 256)
    def _(n):
        tile = pl.ds(pl.multiple_of(n * 256, 256), 256)
        work[:, tile] = mul_nt(ident, img[tile, :])
        maps = jnp.concatenate([mapt[c] for c in range(2 * nj)], axis=1)
        proj[:, tile] = jnp.dot(maps, wide[:, tile], preferred_element_type=F32)

    forward(0)

    lane = lax.broadcasted_iota(jnp.int32, (1, rows), 1)
    who = lane // LPI
    focus = jnp.zeros((1, rows), F32)
    shift_x = jnp.zeros((1, rows), F32)
    shift_y = jnp.zeros((1, rows), F32)
    for p in range(rows // LPI):
        mine = who == p
        focus = jnp.where(mine, dfc[cls[0, p]], focus)
        shift_x = jnp.where(mine, shf[0, 0, p].astype(F32), shift_x)
        shift_y = jnp.where(mine, shf[0, 1, p].astype(F32), shift_y)
    theta = (lane - who * LPI).astype(F32) * (math.pi / LPI)
    along = shift_x * sine(theta + 0.5 * math.pi) + shift_y * sine(theta)
    turn = along * (math.pi / radii)
    subf = sub.astype(F32)
    first = subf * turn
    start_re, start_im = sine(first + 0.5 * math.pi), sine(first)
    eighth = 8.0 * turn
    turn_re, turn_im = sine(eighth + 0.5 * math.pi), sine(eighth)

    def phase_step(q, carry):
        e_re, e_im = carry
        re_rows = pl.ds(pl.multiple_of(8 * q, 8), 8)
        im_rows = pl.ds(pl.multiple_of(radii + 8 * q, 8), 8)
        ratio = (subf + (8 * q).astype(F32)) / radii
        ctf = -sine(CTF_GAIN * focus * (ratio * ratio) + PHASE_ZERO)
        im_re, im_im = work[re_rows, :], work[im_rows, :]
        work[re_rows, :] = ctf * (e_re * im_re + e_im * im_im)
        work[im_rows, :] = ctf * (e_re * im_im - e_im * im_re)
        c2 = ctf * ctf
        square[re_rows, :] = c2
        square[im_rows, :] = c2
        return e_re * turn_re - e_im * turn_im, e_re * turn_im + e_im * turn_re

    half_q = radii // 16
    carry = lax.fori_loop(0, half_q, phase_step, (start_re, start_im))
    forward(1)
    lax.fori_loop(half_q, radii // 8, phase_step, carry)

    for p in range(n_slab - 1):
        tap_copies[p].wait_recv()
        build_matrix(otap.at[p], owide)
        for j in range(nj):
            if p == 0 and j + 2 < nj:
                forward(j + 2)
            y_copies[p][j].wait_recv()
            deep = pl.ds(j * 2 * CHUNK, 2 * CHUNK)
            pairs = jnp.concatenate([omap[p, 2 * j], omap[p, 2 * j + 1]], axis=1)

            @pl.loop(0, rows // 256)
            def _(n):
                tile = pl.ds(pl.multiple_of(n * 256, 256), 256)
                proj[:, tile] += jnp.dot(pairs, owide[deep, tile], preferred_element_type=F32)

    @pl.loop(0, cols // 16)
    def _(q):
        at = pl.ds(pl.multiple_of(16 * q, 16), 16)
        back[at, :] = (square[at, :] * proj[at, :] - work[at, :]).astype(BF16)

    def grad_block(b):
        return mul_nt(back[...], wide[pl.ds(pl.multiple_of(b * bw, bw), bw), :])

    p_copies = []
    for t in range(nz):
        s1send[t] = grad_block(2 * zs[t] + 1 - y).astype(BF16)
        p_copies.append(go(remote(s1send.at[t], s1recv.at[t], p_s.at[t], p_r.at[t], pair)))
    q_copies = []
    for t in range(nz):
        gown[t] = grad_block(2 * zs[t] + y)
    for t in range(nz - 1):
        p_copies[t].wait_recv()
        s2send[t] = (gown[t] + s1recv[t].astype(F32)).astype(BF16)
        q_copies.append(go(remote(s2send.at[t], s2recv.at[t], q_s.at[t], q_r.at[t], zpeers[t])))
    p_copies[nz - 1].wait_recv()
    total = gown[nz - 1] + s1recv[nz - 1].astype(F32)
    for t in range(nz - 1):
        q_copies[t].wait_recv()
        total = total + s2recv[t].astype(F32)
    gall[d] = total.astype(BF16)

    g_copies = [go(remote(gall.at[d], gall.at[d], g_s.at[t], g_r.at[t], zpeers[t])) for t in range(nz - 1)]
    f_copies = [go(remote(gall.at[d], gall.at[d], f_s.at[0], f_r.at[0], pair))]

    mine = vol[pl.ds(pl.multiple_of(d * bw, bw), bw), :]
    high = mine.astype(BF16)
    low = (mine - high.astype(F32)).astype(BF16)
    cand_wide = (mul_nt(ident, high) + mul_nt(ident, low)) - step * total
    cand[...] = cand_wide.astype(BF16)
    c_copy = go(remote(cand, ocand, c_s.at[0], c_r.at[0], other_half))
    c_copy.wait_recv()
    theirs = ocand[...].astype(F32)

    def shell(a, b):
        prod = a * b
        prod = prod[:radii] + prod[radii:]
        prod = jnp.concatenate([prod, prod], axis=0)
        return mul_nt(jnp.ones((8, bw), F32), prod, lax.Precision.HIGHEST)

    fs[0] = jnp.concatenate(
        [shell(cand_wide, theirs), shell(cand_wide, cand_wide), shell(theirs, theirs)], axis=0
    )
    ux = [go(remote(fs.at[0], fx.at[p], ux_s.at[p], ux_r.at[p], peers[p])) for p in range(n_slab - 1)]

    def forward_grad(t):
        g_copies[t].wait_recv()
        source = 2 * lax.rem(z + nz - 1 - t, nz) + y
        f_copies.append(go(remote(gall.at[source], gall.at[source], f_s.at[t + 1], f_r.at[t + 1], pair)))

    forward_grad(0)
    sums = fs[0]
    for p in range(n_slab - 1):
        ux[p].wait_recv()
        sums = sums + fx[p]
    fs[1] = sums
    uy = go(remote(fs.at[1], fy, uy_s.at[0], uy_r.at[0], pair))
    if nz > 2:
        forward_grad(1)
    uy.wait_recv()
    sums = sums + fy[...]
    fs[2] = sums
    uz = [go(remote(fs.at[2], fz.at[t], uz_s.at[t], uz_r.at[t], zpeers[t])) for t in range(nz - 1)]
    for t in range(2, nz - 1):
        forward_grad(t)
    for t in range(nz - 1):
        uz[t].wait_recv()
        sums = sums + fz[t]
    num, den_mine, den_other = sums[0:1], sums[8:9], sums[16:17]
    fsc = num / (jnp.sqrt(den_mine * den_other) + 1e-06)
    factor = step * (1.0 + fsc) / 2.0

    for t in range(nz):
        f_copies[t].wait_recv()
    small = eye(bw, BF16)

    @pl.loop(0, n_dom)
    def _(b):
        at = pl.ds(pl.multiple_of(b * bw, bw), bw)
        out[at, :] = vol[at, :] - factor * mul_nt(small, gall[b])

    for copy in sends:
        copy.wait_send()


def body(n_dom, n_slab, volume, images, tap_index, tap_weight, classes, shifts, defocus):
    slab_map, data = volume[0], images[0]
    lines, cols = slab_map.shape
    rows = data.shape[0]
    depth = tap_index.shape[2]
    step = STEP_SCALE / math.sqrt(rows * n_dom * depth / lines)
    nz, bw = n_dom // 2, lines // n_dom
    nc, np_, nj = lines // CHUNK, n_slab - 1, lines // CHUNK // 2
    dma = pltpu.SemaphoreType.DMA
    vmem = pl.BlockSpec(memory_space=pltpu.VMEM)
    smem = pl.BlockSpec(memory_space=pltpu.SMEM)
    scratch = [
        pltpu.VMEM((nc, cols, CHUNK), BF16),
        pltpu.VMEM((np_, nc, cols, CHUNK), BF16),
        pltpu.VMEM((16, rows), BF16),
        pltpu.VMEM((np_, 16, rows), BF16),
        pltpu.VMEM((lines, rows), BF16),
        pltpu.VMEM((lines, rows), BF16),
        pltpu.VMEM((cols, rows), F32),
        pltpu.VMEM((cols, rows), F32),
        pltpu.VMEM((cols, rows), F32),
        pltpu.VMEM((cols, rows), BF16),
        pltpu.VMEM((nz, cols, bw), F32),
        pltpu.VMEM((nz, cols, bw), BF16),
        pltpu.VMEM((nz, cols, bw), BF16),
        pltpu.VMEM((nz - 1, cols, bw), BF16),
        pltpu.VMEM((nz - 1, cols, bw), BF16),
        pltpu.VMEM((n_dom, cols, bw), BF16),
        pltpu.VMEM((cols, bw), BF16),
        pltpu.VMEM((cols, bw), BF16),
        pltpu.VMEM((3, 24, cols), F32),
        pltpu.VMEM((np_, 24, cols), F32),
        pltpu.VMEM((24, cols), F32),
        pltpu.VMEM((nz - 1, 24, cols), F32),
    ]
    for shape in (
        (np_,), (np_, nj), (np_, nj), (nz,), (nz - 1,), (nz - 1,), (nz,), (1,), (np_,), (1,), (nz - 1,)
    ):
        scratch += [dma(shape), dma(shape)]
    result = pl.pallas_call(
        functools.partial(kernel, n_dom, n_slab, step),
        out_shape=jax.ShapeDtypeStruct((lines, cols), F32),
        in_specs=[vmem] * 4 + [smem] * 3,
        out_specs=vmem,
        scratch_shapes=scratch,
        compiler_params=pltpu.CompilerParams(
            collective_id=0, has_side_effects=True, vmem_limit_bytes=56 * 1024 * 1024
        ),
    )(slab_map, data, tap_index[0, 0], tap_weight[0, 0], classes, shifts, defocus)
    return result[None]


def solution(mesh):
    placed = (
        P("half", "slab", None),
        P("half", "dom", None),
        P("half", "slab", None, "dom"),
        P("half", "slab", None, "dom"),
        P("half", "dom"),
        P("half", None, "dom"),
        P(),
    )
    return jax.shard_map(
        functools.partial(body, mesh.shape["dom"], mesh.shape["slab"]),
        mesh=mesh, in_specs=placed, out_specs=P("half", "slab", None), check_vma=False,
    )
```

time: 326 us -> 66.7 us (0.20)
  waiting for transfers between devices: 138 us -> 0 us
  other arithmetic: 103 us -> 0 us
  Pallas kernels: 0 us -> 59.6 us
  local copies, waits for them, and re-layouts: 51.7 us -> 6.94 us
  blocking collectives: 19.3 us -> 0 us
  between operations: 13.7 us -> 0.01 us
    psum x1 -> x0, waiting for transfers between devices: 102 us -> none  [body(): grad = lax.psum(local_grad, 'dom')]
    scatter-add x8 -> x0, other arithmetic: 78.5 us -> none  [spread_back(): total.at[local].add(taps_wide[tap_num][:, None] * back_wide, mode='drop')]
    pallas_call x0 -> x1, Pallas kernels: none -> 59.6 us  [body(): pl.pallas_call(functools.partial(kernel, n_dom, n_slab, step), out_shape=...]
    gather x8 -> x0, local copies, waits for them, and re-layouts: 39.4 us -> none  [body(): picked = jnp.take(map_low, taps_at[tap_num], axis=0)]
    reduce_scatter x1 -> x0, waiting for transfers between devices: 33.1 us -> none  [body(): lax.psum_scatter(partial_value, 'slab', scatter_dimension=0, tiled=True)]
    all_gather x1 -> x0, blocking collectives: 14.3 us -> none  [body(): back = lax.all_gather(back_share, 'slab', axis=0, tiled=True)]
    add x2 -> x0, other arithmetic: 8.27 us -> none  [the longest x1 8.19 us: body(): partial_value + taps_wide[tap_num][:, None] * picked.astype(jnp.float32)]
    convert_element_type x6 -> x0, other arithmetic: 7.27 us -> none  [the longest x2 5.41 us: body(): other = swapped(cand.astype(jnp.bfloat16), 'half', 0).astype(cand.dtype)]
  transfers between devices with their start and end apart: 3 -> 0, of which waited for: 3 -> 0; matrix products, arithmetic and copies ran while one was open for 0% -> 0% of each run, Pallas kernels for 0% -> 0%
where the time goes in v1:
time: 66.7 us; the launch traced here: 66.6 us
  Pallas kernels  59.6 us (89%)
  local copies, waits for them, and re-layouts  6.94 us (10%)
    pallas_call x1, Pallas kernels, body(): pl.pallas_call(functools.partial(kernel, n_dom, n_slab, step), out_shape=...  59.6 us
    unnamed x4, local copies, waits for them, and re-layouts  4.19 us
    broadcast_in_dim x1, local copies, waits for them, and re-layouts, body(): return result[None]  2.75 us

profile of v1, /device:TPU:0, one launch (start us, length us, event | category | flops | bytes accessed | tf_op | source)
XLA Modules:
  0.0 66.6 jit_solution(13881613102437705030)
XLA Ops:
  0.0 0.0 copy-start
  0.0 2.3 %copy.9 = bf16[1,1024,400]{2,1,0:T(8,128)(2,1)} copy(bf16[1,1024,400]{1,2,0:T(8,128)(2,1)} %param.8) | data formatting | bytes 1638400 | tf_op args[1]
  2.3 0.0 copy-done
  2.4 1.8 %copy.8 = f32[1,1024,400]{2,1,0:T(8,128)} copy(f32[1,1024,400]{1,2,0:T(8,128)S(1)} %copy-done) | data formatting | bytes 3276800 | tf_op args[0]
  4.2 59.6 %shard_map.73 = f32[1024,400]{1,0:T(8,128)} custom-call(f32[1024,400]{1,0:T(8,128)} %bitcast.6, bf16[1024,400]{1,0:T(8,128)(2,1)} %bitcast.7, s32[8,1024]{1,0:T(8,128)} %bitcast.8, f32[8,1024]{1,0:T(8,128)} %bitcast.9, s32[1,16]{1,0:T(1,128)} %cls.1, s32[1,2,16]{2,1,0:T(2,128)} %shf.1, f32[16]{0:T(128)} %dfc.1), custom_call_target="tpu_custom_call" | custom-call | tf_op jit(solution)/shard_map/pallas_call | solution.py:325
  63.8 2.7 %copy.10 = f32[1,1024,400]{1,2,0:T(8,128)} copy(f32[1,1024,400]{2,1,0:T(8,128)} %bitcast.5) | data formatting | bytes 3276800 | tf_op jit(solution)/shard_map/broadcast_in_dim | solution.py:335
Async XLA Ops:
  0.0 2.4 %copy-start = (f32[1,1024,400]{1,2,0:T(8,128)S(1)}, f32[1,1024,400]{1,2,0:T(8,128)}, u32[]{:S(2)}) copy-start(f32[1,1024,400]{1,2,0:T(8,128)} %param.7) | copy-start | bytes 4915204

commit v2 on v1

--- a/solution.py
+++ b/solution.py
@@ -41,6 +41,12 @@
     return jnp.where(row == col, 1.0, 0.0).astype(kind)
 
 
+def placing(n, offset):
+    row = lax.broadcasted_iota(jnp.int32, (n, CHUNK), 0)
+    col = lax.broadcasted_iota(jnp.int32, (n, CHUNK), 1)
+    return jnp.where(row + offset == col, 1.0, 0.0).astype(BF16)
+
+
 def remote(src, dst, send, recv, where):
     return pltpu.make_async_remote_copy(
         src_ref=src, dst_ref=dst, send_sem=send, recv_sem=recv, device_id=where, device_id_type=MESH
@@ -66,13 +72,13 @@
     out,
     mapt, omap, ptap, otap, wide, owide, work, proj, square, back,
     gown, s1send, s1recv, s2send, s2recv, gall, cand, ocand, fs, fx, fy, fz,
-    tap_s, tap_r, x_s, x_r, y_s, y_r, p_s, p_r, q_s, q_r, g_s, g_r, f_s, f_r, c_s, c_r,
+    tap_s, tap_r, x_s, x_r, y_s, y_r, z_s, z_r, p_s, p_r, q_s, q_r, g_s, g_r, f_s, f_r, c_s, c_r,
     ux_s, ux_r, uy_s, uy_r, uz_s, uz_r,
 ):
     h, d, s = lax.axis_index("half"), lax.axis_index("dom"), lax.axis_index("slab")
-    lines, cols = vol.shape
+    cols, lines = vol.shape
     radii = cols // 2
-    rows = img.shape[0]
+    rows = img.shape[1]
     nz = n_dom // 2
     y, z = lax.rem(d, 2), d // 2
     pair = (h, d + 1 - 2 * y, s)
@@ -81,7 +87,10 @@
     zs = [lax.rem(z + 1 + t, nz) for t in range(nz)]
     zpeers = [(h, 2 * zs[t] + y, s) for t in range(nz - 1)]
     bw = lines // n_dom
-    nj = lines // CHUNK // 2
+    quarter = lines // CHUNK // 4
+    zpair = (h, d + 2 - 4 * lax.rem(z, 2), s)
+    mine_q = 2 * lax.rem(z, 2) + y
+    y_q, z_q, diag_q = mine_q + 1 - 2 * y, mine_q + 2 - 4 * lax.rem(z, 2), 3 - mine_q
 
     barrier = pltpu.get_barrier_semaphore()
     everyone = [pair, other_half] + peers + zpeers
@@ -98,13 +107,9 @@
         block = jnp.where(hit, lax.shift_right_logical(line, 3).astype(F32), block)
     ptap[...] = jnp.concatenate([value, block], axis=0).astype(BF16)
 
-    ident = eye(cols, BF16)
-
-    def map_chunk(c):
-        part = vol[pl.ds(pl.multiple_of(c * CHUNK, CHUNK), CHUNK), :].astype(BF16)
-        mapt[c] = mul_nt(ident, part).astype(BF16)
-
-    pl.loop(0, 2 * nj)(map_chunk)
+    @pl.loop(0, lines // CHUNK)
+    def _(c):
+        mapt[c] = vol[:, pl.ds(pl.multiple_of(c * CHUNK, CHUNK), CHUNK)].astype(BF16)
 
     pl.semaphore_wait(barrier, len(everyone))
     sends = []
@@ -117,26 +122,28 @@
     tap_copies = [go(remote(ptap, otap.at[p], tap_s.at[p], tap_r.at[p], peers[p])) for p in range(n_slab - 1)]
     x_copies = [
         [
-            go(remote(mapt.at[2 * j + y], omap.at[p, 2 * j + y], x_s.at[p, j], x_r.at[p, j], peers[p]))
-            for j in range(nj)
+            go(remote(mapt.at[c], omap.at[p, c], x_s.at[p, i], x_r.at[p, i], peers[p]))
+            for i, c in enumerate([g * quarter + u for g in (mine_q, diag_q) for u in range(quarter)])
         ]
         for p in range(n_slab - 1)
     ]
-    y_copies = [[None] * nj for p in range(n_slab - 1)]
-
-    def forward(j):
+    y_copies = [[None] * quarter for p in range(n_slab - 1)]
+    z_copies = [[None] * quarter for p in range(n_slab - 1)]
+
+    def forward(u):
         for p in range(n_slab - 1):
-            x_copies[p][j].wait_recv()
-            slot = omap.at[p, 2 * j + y]
-            y_copies[p][j] = go(remote(slot, slot, y_s.at[p, j], y_r.at[p, j], pair))
+            x_copies[p][u].wait_recv()
+            slot = omap.at[p, mine_q * quarter + u]
+            y_copies[p][u] = go(remote(slot, slot, y_s.at[p, u], y_r.at[p, u], pair))
+            z_copies[p][u] = go(remote(slot, slot, z_s.at[p, u], z_r.at[p, u], zpair))
 
     build_matrix(ptap, wide)
 
     @pl.loop(0, rows // 256)
     def _(n):
         tile = pl.ds(pl.multiple_of(n * 256, 256), 256)
-        work[:, tile] = mul_nt(ident, img[tile, :])
-        maps = jnp.concatenate([mapt[c] for c in range(2 * nj)], axis=1)
+        work[:, tile] = img[:, tile].astype(F32)
+        maps = jnp.concatenate([mapt[c] for c in range(4 * quarter)], axis=1)
         proj[:, tile] = jnp.dot(maps, wide[:, tile], preferred_element_type=F32)
 
     forward(0)
@@ -176,23 +183,26 @@
 
     half_q = radii // 16
     carry = lax.fori_loop(0, half_q, phase_step, (start_re, start_im))
-    forward(1)
+    for u in range(1, quarter):
+        forward(u)
     lax.fori_loop(half_q, radii // 8, phase_step, carry)
 
     for p in range(n_slab - 1):
         tap_copies[p].wait_recv()
         build_matrix(otap.at[p], owide)
-        for j in range(nj):
-            if p == 0 and j + 2 < nj:
-                forward(j + 2)
-            y_copies[p][j].wait_recv()
-            deep = pl.ds(j * 2 * CHUNK, 2 * CHUNK)
-            pairs = jnp.concatenate([omap[p, 2 * j], omap[p, 2 * j + 1]], axis=1)
+        for g, copies in (
+            (mine_q, []), (y_q, y_copies[p]), (z_q, z_copies[p]), (diag_q, x_copies[p][quarter:])
+        ):
+            for copy in copies:
+                copy.wait_recv()
+            depth = quarter * CHUNK
+            deep = pl.ds(pl.multiple_of(g * depth, depth), depth)
+            maps = jnp.concatenate([omap[p, g * quarter + u] for u in range(quarter)], axis=1)
 
             @pl.loop(0, rows // 256)
             def _(n):
                 tile = pl.ds(pl.multiple_of(n * 256, 256), 256)
-                proj[:, tile] += jnp.dot(pairs, owide[deep, tile], preferred_element_type=F32)
+                proj[:, tile] += jnp.dot(maps, owide[deep, tile], preferred_element_type=F32)
 
     @pl.loop(0, cols // 16)
     def _(q):
@@ -223,10 +233,16 @@
     g_copies = [go(remote(gall.at[d], gall.at[d], g_s.at[t], g_r.at[t], zpeers[t])) for t in range(nz - 1)]
     f_copies = [go(remote(gall.at[d], gall.at[d], f_s.at[0], f_r.at[0], pair))]
 
-    mine = vol[pl.ds(pl.multiple_of(d * bw, bw), bw), :]
-    high = mine.astype(BF16)
-    low = (mine - high.astype(F32)).astype(BF16)
-    cand_wide = (mul_nt(ident, high) + mul_nt(ident, low)) - step * total
+    if bw % CHUNK == 0:
+        mine = vol[:, pl.ds(pl.multiple_of(d * bw, CHUNK), bw)]
+    else:
+        at = (d * bw) // CHUNK
+        near = vol[:, pl.ds(pl.multiple_of(at * CHUNK, CHUNK), CHUNK)]
+        high = near.astype(BF16)
+        low = (near - high.astype(F32)).astype(BF16)
+        pick = placing(bw, d * bw - at * CHUNK)
+        mine = mul_nt(high, pick) + mul_nt(low, pick)
+    cand_wide = mine - step * total
     cand[...] = cand_wide.astype(BF16)
     c_copy = go(remote(cand, ocand, c_s.at[0], c_r.at[0], other_half))
     c_copy.wait_recv()
@@ -235,12 +251,11 @@
     def shell(a, b):
         prod = a * b
         prod = prod[:radii] + prod[radii:]
-        prod = jnp.concatenate([prod, prod], axis=0)
         return mul_nt(jnp.ones((8, bw), F32), prod, lax.Precision.HIGHEST)
 
-    fs[0] = jnp.concatenate(
-        [shell(cand_wide, theirs), shell(cand_wide, cand_wide), shell(theirs, theirs)], axis=0
-    )
+    kind = lax.broadcasted_iota(jnp.int32, (8, radii), 0)
+    den_mine, den_other = shell(cand_wide, cand_wide), shell(theirs, theirs)
+    fs[0] = jnp.where(kind == 0, shell(cand_wide, theirs), jnp.where(kind == 1, den_mine, den_other))
     ux = [go(remote(fs.at[0], fx.at[p], ux_s.at[p], ux_r.at[p], peers[p])) for p in range(n_slab - 1)]
 
     def forward_grad(t):
@@ -266,31 +281,42 @@
     for t in range(nz - 1):
         uz[t].wait_recv()
         sums = sums + fz[t]
-    num, den_mine, den_other = sums[0:1], sums[8:9], sums[16:17]
+    num, den_mine, den_other = sums[0:1], sums[1:2], sums[2:3]
     fsc = num / (jnp.sqrt(den_mine * den_other) + 1e-06)
     factor = step * (1.0 + fsc) / 2.0
+    column = jnp.sum(eye(radii, F32) * factor, axis=1, keepdims=True)
+    column = jnp.concatenate([column, column], axis=0)
 
     for t in range(nz):
         f_copies[t].wait_recv()
-    small = eye(bw, BF16)
-
-    @pl.loop(0, n_dom)
-    def _(b):
-        at = pl.ds(pl.multiple_of(b * bw, bw), bw)
-        out[at, :] = vol[at, :] - factor * mul_nt(small, gall[b])
+    if bw % CHUNK == 0:
+        @pl.loop(0, n_dom)
+        def _(b):
+            at = pl.ds(pl.multiple_of(b * bw, CHUNK), bw)
+            out[:, at] = vol[:, at] - column * gall[b].astype(F32)
+    else:
+        share = CHUNK // bw
+
+        @pl.loop(0, lines // CHUNK)
+        def _(c):
+            at = pl.ds(pl.multiple_of(c * CHUNK, CHUNK), CHUNK)
+            whole = jnp.zeros((cols, CHUNK), F32)
+            for u in range(share):
+                whole = whole + jnp.dot(gall[c * share + u], placing(bw, u * bw), preferred_element_type=F32)
+            out[:, at] = vol[:, at] - column * whole
 
     for copy in sends:
         copy.wait_send()
 
 
 def body(n_dom, n_slab, volume, images, tap_index, tap_weight, classes, shifts, defocus):
-    slab_map, data = volume[0], images[0]
-    lines, cols = slab_map.shape
-    rows = data.shape[0]
+    slab_map, data = volume[0].T, images[0].T
+    cols, lines = slab_map.shape
+    rows = data.shape[1]
     depth = tap_index.shape[2]
     step = STEP_SCALE / math.sqrt(rows * n_dom * depth / lines)
     nz, bw = n_dom // 2, lines // n_dom
-    nc, np_, nj = lines // CHUNK, n_slab - 1, lines // CHUNK // 2
+    nc, np_, nq = lines // CHUNK, n_slab - 1, lines // CHUNK // 4
     dma = pltpu.SemaphoreType.DMA
     vmem = pl.BlockSpec(memory_space=pltpu.VMEM)
     smem = pl.BlockSpec(memory_space=pltpu.SMEM)
@@ -313,18 +339,18 @@
         pltpu.VMEM((n_dom, cols, bw), BF16),
         pltpu.VMEM((cols, bw), BF16),
         pltpu.VMEM((cols, bw), BF16),
-        pltpu.VMEM((3, 24, cols), F32),
-        pltpu.VMEM((np_, 24, cols), F32),
-        pltpu.VMEM((24, cols), F32),
-        pltpu.VMEM((nz - 1, 24, cols), F32),
+        pltpu.VMEM((3, 8, cols // 2), F32),
+        pltpu.VMEM((np_, 8, cols // 2), F32),
+        pltpu.VMEM((8, cols // 2), F32),
+        pltpu.VMEM((nz - 1, 8, cols // 2), F32),
     ]
     for shape in (
-        (np_,), (np_, nj), (np_, nj), (nz,), (nz - 1,), (nz - 1,), (nz,), (1,), (np_,), (1,), (nz - 1,)
+        (np_,), (np_, 2 * nq), (np_, nq), (np_, nq), (nz,), (nz - 1,), (nz - 1,), (nz,), (1,), (np_,), (1,), (nz - 1,)
     ):
         scratch += [dma(shape), dma(shape)]
     result = pl.pallas_call(
         functools.partial(kernel, n_dom, n_slab, step),
-        out_shape=jax.ShapeDtypeStruct((lines, cols), F32),
+        out_shape=jax.ShapeDtypeStruct((cols, lines), F32),
         in_specs=[vmem] * 4 + [smem] * 3,
         out_specs=vmem,
         scratch_shapes=scratch,
@@ -332,7 +358,7 @@
             collective_id=0, has_side_effects=True, vmem_limit_bytes=56 * 1024 * 1024
         ),
     )(slab_map, data, tap_index[0, 0], tap_weight[0, 0], classes, shifts, defocus)
-    return result[None]
+    return result.T[None]
 
 
 def solution(mesh):

time: 66.7 us -> 56 us (0.84)
  Pallas kernels: 59.6 us -> 53 us
  local copies, waits for them, and re-layouts: 6.94 us -> 2.78 us
    pallas_call x1, Pallas kernels: 59.6 us -> 53 us  [body(): pl.pallas_call(functools.partial(kernel, n_dom, n_slab, step), out_shape=...]
    broadcast_in_dim x1 -> x0, local copies, waits for them, and re-layouts: 2.75 us -> none  [body(): return result[None]]
    unnamed x4 -> x1, local copies, waits for them, and re-layouts: 4.19 us -> 2.78 us
where the time goes in v2:
time: 56 us; the launch traced here: 55.8 us
  Pallas kernels  53 us (95%)
  local copies, waits for them, and re-layouts  2.78 us (5%)
    pallas_call x1, Pallas kernels, body(): pl.pallas_call(functools.partial(kernel, n_dom, n_slab, step), out_shape=...  53 us
    unnamed x1, local copies, waits for them, and re-layouts  2.78 us

profile of v2, /device:TPU:0, one launch (start us, length us, event | category | flops | bytes accessed | tf_op | source)
XLA Modules:
  0.0 55.8 jit_solution(17357678915223313429)
XLA Ops:
  0.0 53.0 %shard_map.73 = f32[400,1024]{1,0:T(8,128)} custom-call(f32[400,1024]{1,0:T(8,128)} %bitcast.12, bf16[400,1024]{1,0:T(8,128)(2,1)} %bitcast.13, s32[8,1024]{1,0:T(8,128)} %bitcast.14, f32[8,1024]{1,0:T(8,128)} %bitcast.15, s32[1,16]{1,0:T(1,128)} %cls.1, s32[1,2,16]{2,1,0:T(2,128)} %shf.1, f32[16]{0:T(128)} %dfc.1), custom_call_target="tpu_custom_call" | custom-call | tf_op jit(solution)/shard_map/pallas_call | solution.py:351
  53.1 2.8 %copy.9 = f32[1,1024,400]{1,2,0:T(8,128)} copy(f32[1,1024,400]{1,2,0:T(8,128)} %bitcast.11) | data formatting | bytes 3276800

commit v3 on v2

--- a/solution.py
+++ b/solution.py
@@ -114,9 +114,12 @@
     pl.semaphore_wait(barrier, len(everyone))
     sends = []
 
-    def go(copy):
-        copy.start()
-        sends.append(copy)
+    def go(copy, needed=None):
+        if needed is None:
+            copy.start()
+        else:
+            pl.when(needed)(copy.start)
+        sends.append((copy, needed))
         return copy
 
     tap_copies = [go(remote(ptap, otap.at[p], tap_s.at[p], tap_r.at[p], peers[p])) for p in range(n_slab - 1)]
@@ -138,6 +141,7 @@
             z_copies[p][u] = go(remote(slot, slot, z_s.at[p, u], z_r.at[p, u], zpair))
 
     build_matrix(ptap, wide)
+    forward(0)
 
     @pl.loop(0, rows // 256)
     def _(n):
@@ -146,7 +150,8 @@
         maps = jnp.concatenate([mapt[c] for c in range(4 * quarter)], axis=1)
         proj[:, tile] = jnp.dot(maps, wide[:, tile], preferred_element_type=F32)
 
-    forward(0)
+    for u in range(1, quarter):
+        forward(u)
 
     lane = lax.broadcasted_iota(jnp.int32, (1, rows), 1)
     who = lane // LPI
@@ -181,11 +186,7 @@
         square[im_rows, :] = c2
         return e_re * turn_re - e_im * turn_im, e_re * turn_im + e_im * turn_re
 
-    half_q = radii // 16
-    carry = lax.fori_loop(0, half_q, phase_step, (start_re, start_im))
-    for u in range(1, quarter):
-        forward(u)
-    lax.fori_loop(half_q, radii // 8, phase_step, carry)
+    lax.fori_loop(0, radii // 8, phase_step, (start_re, start_im))
 
     for p in range(n_slab - 1):
         tap_copies[p].wait_recv()
@@ -230,8 +231,39 @@
         total = total + s2recv[t].astype(F32)
     gall[d] = total.astype(BF16)
 
-    g_copies = [go(remote(gall.at[d], gall.at[d], g_s.at[t], g_r.at[t], zpeers[t])) for t in range(nz - 1)]
-    f_copies = [go(remote(gall.at[d], gall.at[d], f_s.at[0], f_r.at[0], pair))]
+    middle = cols // 32 * 16
+    parts = ((0, middle), (middle, cols - middle))
+    to_right, to_left = (h, d + 2, s), (h, d - 2, s)
+
+    def share(zz, u):
+        return gall.at[2 * zz + y, pl.ds(*parts[u]), :]
+
+    def relay(k, u):
+        for way, where, source, needed in (
+            (0, to_right, z - k, jnp.logical_and(z - k >= 0, z + 1 < nz)),
+            (1, to_left, z + k, jnp.logical_and(z + k < nz, z >= 1)),
+        ):
+            part = share(source, u)
+            go(remote(part, part, g_s.at[way, k, u], g_r.at[way, k, u], where), needed)
+
+    def from_pair(way, k, u, source, needed):
+        part = share(source, u)
+        pair_copies.append((go(remote(part, part, f_s.at[way, k, u], f_r.at[way, k, u], pair), needed), needed))
+
+    pair_copies = []
+    for u in range(2):
+        relay(0, u)
+        from_pair(0, 0, u, z, None)
+
+    def arrive(k):
+        for u in range(2):
+            for way, source, needed in ((0, z - k, z - k >= 0), (1, z + k, z + k < nz)):
+                part = share(source, u)
+                come = remote(part, part, g_s.at[way, k - 1, u], g_r.at[way, k - 1, u], pair)
+                pl.when(needed)(come.wait_recv)
+                from_pair(way, k, u, source, needed)
+            if k < nz - 1:
+                relay(k, u)
 
     if bw % CHUNK == 0:
         mine = vol[:, pl.ds(pl.multiple_of(d * bw, CHUNK), bw)]
@@ -258,12 +290,7 @@
     fs[0] = jnp.where(kind == 0, shell(cand_wide, theirs), jnp.where(kind == 1, den_mine, den_other))
     ux = [go(remote(fs.at[0], fx.at[p], ux_s.at[p], ux_r.at[p], peers[p])) for p in range(n_slab - 1)]
 
-    def forward_grad(t):
-        g_copies[t].wait_recv()
-        source = 2 * lax.rem(z + nz - 1 - t, nz) + y
-        f_copies.append(go(remote(gall.at[source], gall.at[source], f_s.at[t + 1], f_r.at[t + 1], pair)))
-
-    forward_grad(0)
+    arrive(1)
     sums = fs[0]
     for p in range(n_slab - 1):
         ux[p].wait_recv()
@@ -271,13 +298,13 @@
     fs[1] = sums
     uy = go(remote(fs.at[1], fy, uy_s.at[0], uy_r.at[0], pair))
     if nz > 2:
-        forward_grad(1)
+        arrive(2)
     uy.wait_recv()
     sums = sums + fy[...]
     fs[2] = sums
     uz = [go(remote(fs.at[2], fz.at[t], uz_s.at[t], uz_r.at[t], zpeers[t])) for t in range(nz - 1)]
-    for t in range(2, nz - 1):
-        forward_grad(t)
+    for k in range(3, nz):
+        arrive(k)
     for t in range(nz - 1):
         uz[t].wait_recv()
         sums = sums + fz[t]
@@ -287,26 +314,29 @@
     column = jnp.sum(eye(radii, F32) * factor, axis=1, keepdims=True)
     column = jnp.concatenate([column, column], axis=0)
 
-    for t in range(nz):
-        f_copies[t].wait_recv()
+    for copy, needed in pair_copies:
+        if needed is None:
+            copy.wait_recv()
+        else:
+            pl.when(needed)(copy.wait_recv)
     if bw % CHUNK == 0:
-        @pl.loop(0, n_dom)
-        def _(b):
-            at = pl.ds(pl.multiple_of(b * bw, CHUNK), bw)
-            out[:, at] = vol[:, at] - column * gall[b].astype(F32)
+        for b in range(n_dom):
+            out[:, b * bw:(b + 1) * bw] = column * gall[b].astype(F32)
     else:
-        share = CHUNK // bw
+        fold = CHUNK // bw
 
         @pl.loop(0, lines // CHUNK)
         def _(c):
-            at = pl.ds(pl.multiple_of(c * CHUNK, CHUNK), CHUNK)
             whole = jnp.zeros((cols, CHUNK), F32)
-            for u in range(share):
-                whole = whole + jnp.dot(gall[c * share + u], placing(bw, u * bw), preferred_element_type=F32)
-            out[:, at] = vol[:, at] - column * whole
-
-    for copy in sends:
-        copy.wait_send()
+            for u in range(fold):
+                whole = whole + jnp.dot(gall[c * fold + u], placing(bw, u * bw), preferred_element_type=F32)
+            out[:, pl.ds(pl.multiple_of(c * CHUNK, CHUNK), CHUNK)] = column * whole
+
+    for copy, needed in sends:
+        if needed is None:
+            copy.wait_send()
+        else:
+            pl.when(needed)(copy.wait_send)
 
 
 def body(n_dom, n_slab, volume, images, tap_index, tap_weight, classes, shifts, defocus):
@@ -345,10 +375,10 @@
         pltpu.VMEM((nz - 1, 8, cols // 2), F32),
     ]
     for shape in (
-        (np_,), (np_, 2 * nq), (np_, nq), (np_, nq), (nz,), (nz - 1,), (nz - 1,), (nz,), (1,), (np_,), (1,), (nz - 1,)
+        (np_,), (np_, 2 * nq), (np_, nq), (np_, nq), (nz,), (nz - 1,), (2, nz - 1, 2), (2, nz, 2), (1,), (np_,), (1,), (nz - 1,)
     ):
         scratch += [dma(shape), dma(shape)]
-    result = pl.pallas_call(
+    change = pl.pallas_call(
         functools.partial(kernel, n_dom, n_slab, step),
         out_shape=jax.ShapeDtypeStruct((cols, lines), F32),
         in_specs=[vmem] * 4 + [smem] * 3,
@@ -358,7 +388,7 @@
             collective_id=0, has_side_effects=True, vmem_limit_bytes=56 * 1024 * 1024
         ),
     )(slab_map, data, tap_index[0, 0], tap_weight[0, 0], classes, shifts, defocus)
-    return result.T[None]
+    return (slab_map - change).T[None]
 
 
 def solution(mesh):

time: 56 us -> 54.2 us (0.968)
  other arithmetic: 0 us -> 2.98 us
  local copies, waits for them, and re-layouts: 2.78 us -> 0.01 us
  Pallas kernels: 53 us -> 51 us
    broadcast_in_dim x0 -> x1, other arithmetic: none -> 2.98 us  [body(): return (slab_map - change).T[None]]
    unnamed x1 -> x2, local copies, waits for them, and re-layouts: 2.78 us -> 0.01 us
    pallas_call x1, Pallas kernels: 53 us -> 51 us  [body(): pl.pallas_call(functools.partial(kernel, n_dom, n_slab, step), out_shape=...]
where the time goes in v3:
time: 54.2 us; the launch traced here: 54 us
  Pallas kernels  51 us (94%)
  other arithmetic  2.98 us (5%)
    pallas_call x1, Pallas kernels, body(): pl.pallas_call(functools.partial(kernel, n_dom, n_slab, step), out_shape=...  51 us
    broadcast_in_dim x1, other arithmetic, body(): return (slab_map - change).T[None]  2.98 us

profile of v3, /device:TPU:0, one launch (start us, length us, event | category | flops | bytes accessed | tf_op | source)
XLA Modules:
  0.0 54.0 jit_solution(12386845000643316554)
XLA Ops:
  0.0 0.0 copy-start
  0.0 51.0 %shard_map.73 = f32[400,1024]{1,0:T(8,128)} custom-call(f32[400,1024]{1,0:T(8,128)} %bitcast.13, bf16[400,1024]{1,0:T(8,128)(2,1)} %bitcast.14, s32[8,1024]{1,0:T(8,128)} %bitcast.15, f32[8,1024]{1,0:T(8,128)} %bitcast.16, s32[1,16]{1,0:T(1,128)} %cls.1, s32[1,2,16]{2,1,0:T(2,128)} %shf.1, f32[16]{0:T(128)} %dfc.1), custom_call_target="tpu_custom_call" | custom-call | tf_op jit(solution)/shard_map/pallas_call | solution.py:381
  51.0 0.0 copy-done
  51.0 3.0 %subtract_bitcast_fusion = f32[1,1024,400]{1,2,0:T(8,128)} fusion(f32[400,1024]{1,0:T(8,128)} %shard_map.73, f32[1,1024,400]{1,2,0:T(8,128)S(1)} %copy-done), kind=kLoop, calls=%fused_computation | loop fusion | flops 409600 | bytes 4915200 | tf_op jit(solution)/shard_map/broadcast_in_dim | solution.py:391
Async XLA Ops:
  0.0 51.0 %copy-start = (f32[1,1024,400]{1,2,0:T(8,128)S(1)}, f32[1,1024,400]{1,2,0:T(8,128)}, u32[]{:S(2)}) copy-start(f32[1,1024,400]{1,2,0:T(8,128)} %param.7) | copy-start | bytes 4915204

commit v4 on v3

--- a/solution.py
+++ b/solution.py
@@ -213,30 +213,39 @@
     def grad_block(b):
         return mul_nt(back[...], wide[pl.ds(pl.multiple_of(b * bw, bw), bw), :])
 
+    middle = cols // 32 * 16
+    parts = ((0, middle), (middle, cols - middle))
+    spans = [pl.ds(*part) for part in parts]
     p_copies = []
     for t in range(nz):
         s1send[t] = grad_block(2 * zs[t] + 1 - y).astype(BF16)
-        p_copies.append(go(remote(s1send.at[t], s1recv.at[t], p_s.at[t], p_r.at[t], pair)))
+        p_copies.append([
+            go(remote(s1send.at[t, span, :], s1recv.at[t, span, :], p_s.at[t, u], p_r.at[t, u], pair))
+            for u, span in enumerate(spans)
+        ])
     q_copies = []
-    for t in range(nz):
+    for t in range(nz - 1):
         gown[t] = grad_block(2 * zs[t] + y)
+        for u, span in enumerate(spans):
+            p_copies[t][u].wait_recv()
+            s2send[t, span, :] = (gown[t, span, :] + s1recv[t, span, :].astype(F32)).astype(BF16)
+            q_copies.append(
+                go(remote(s2send.at[t, span, :], s2recv.at[t, span, :], q_s.at[t, u], q_r.at[t, u], zpeers[t]))
+            )
+    gown[nz - 1] = grad_block(2 * zs[nz - 1] + y)
+    for copy in p_copies[nz - 1]:
+        copy.wait_recv()
+    total = gown[nz - 1] + s1recv[nz - 1].astype(F32)
+    for copy in q_copies:
+        copy.wait_recv()
     for t in range(nz - 1):
-        p_copies[t].wait_recv()
-        s2send[t] = (gown[t] + s1recv[t].astype(F32)).astype(BF16)
-        q_copies.append(go(remote(s2send.at[t], s2recv.at[t], q_s.at[t], q_r.at[t], zpeers[t])))
-    p_copies[nz - 1].wait_recv()
-    total = gown[nz - 1] + s1recv[nz - 1].astype(F32)
-    for t in range(nz - 1):
-        q_copies[t].wait_recv()
         total = total + s2recv[t].astype(F32)
     gall[d] = total.astype(BF16)
 
-    middle = cols // 32 * 16
-    parts = ((0, middle), (middle, cols - middle))
     to_right, to_left = (h, d + 2, s), (h, d - 2, s)
 
     def share(zz, u):
-        return gall.at[2 * zz + y, pl.ds(*parts[u]), :]
+        return gall.at[2 * zz + y, spans[u], :]
 
     def relay(k, u):
         for way, where, source, needed in (
@@ -375,7 +384,7 @@
         pltpu.VMEM((nz - 1, 8, cols // 2), F32),
     ]
     for shape in (
-        (np_,), (np_, 2 * nq), (np_, nq), (np_, nq), (nz,), (nz - 1,), (2, nz - 1, 2), (2, nz, 2), (1,), (np_,), (1,), (nz - 1,)
+        (np_,), (np_, 2 * nq), (np_, nq), (np_, nq), (nz, 2), (nz - 1, 2), (2, nz - 1, 2), (2, nz, 2), (1,), (np_,), (1,), (nz - 1,)
     ):
         scratch += [dma(shape), dma(shape)]
     change = pl.pallas_call(
@@ -385,7 +394,7 @@
         out_specs=vmem,
         scratch_shapes=scratch,
         compiler_params=pltpu.CompilerParams(
-            collective_id=0, has_side_effects=True, vmem_limit_bytes=56 * 1024 * 1024
+            collective_id=0, has_side_effects=True, vmem_limit_bytes=30 * 1024 * 1024
         ),
     )(slab_map, data, tap_index[0, 0], tap_weight[0, 0], classes, shifts, defocus)
     return (slab_map - change).T[None]

time: 54.2 us -> 56.1 us (1.035)
  local copies, waits for them, and re-layouts: 0.01 us -> 6.08 us
  Pallas kernels: 51 us -> 48.2 us
  other arithmetic: 2.98 us -> 1.44 us
    unnamed x2 -> x14, local copies, waits for them, and re-layouts: 0.01 us -> 6.08 us
    pallas_call x1, Pallas kernels: 51 us -> 48.2 us  [body(): pl.pallas_call(functools.partial(kernel, n_dom, n_slab, step), out_shape=...]
    broadcast_in_dim x1, other arithmetic: 2.98 us -> 1.44 us  [body(): return (slab_map - change).T[None]]
where the time goes in v4:
time: 56.1 us; the launch traced here: 55.7 us
  Pallas kernels  48.2 us (86%)
  local copies, waits for them, and re-layouts  6.08 us (11%)
  other arithmetic  1.44 us (3%)
    pallas_call x1, Pallas kernels, body(): pl.pallas_call(functools.partial(kernel, n_dom, n_slab, step), out_shape=...  48.2 us
    unnamed x14, local copies, waits for them, and re-layouts  6.08 us
    broadcast_in_dim x1, other arithmetic, body(): return (slab_map - change).T[None]  1.44 us

profile of v4, /device:TPU:0, one launch (start us, length us, event | category | flops | bytes accessed | tf_op | source)
XLA Modules:
  0.0 55.7 jit_solution(7219620084239334363)
XLA Ops:
  0.0 0.0 copy-start
  0.0 1.4 %copy-done = f32[1,1024,400]{1,2,0:T(8,128)S(1)} copy-done((f32[1,1024,400]{1,2,0:T(8,128)S(1)}, f32[1,1024,400]{1,2,0:T(8,128)}, u32[]{:S(2)}) %copy-start) | copy-done | bytes 1638424
  1.4 0.0 copy-start.1
  1.4 1.1 %copy-done.1 = bf16[1,1024,400]{1,2,0:T(8,128)(2,1)S(1)} copy-done((bf16[1,1024,400]{1,2,0:T(8,128)(2,1)S(1)}, bf16[1,1024,400]{1,2,0:T(8,128)(2,1)}, u32[]{:S(2)}) %copy-start.1) | copy-done | bytes 819224
  2.6 0.0 copy-start.2
  2.6 0.8 %copy-done.2 = s32[1,1,8,1024]{3,2,1,0:T(8,128)S(1)} copy-done((s32[1,1,8,1024]{3,2,1,0:T(8,128)S(1)}, s32[1,1,8,1024]{3,2,1,0:T(8,128)}, u32[]{:S(2)}) %copy-start.2) | copy-done | bytes 32792
  3.3 0.0 copy-start.3
  3.3 0.8 %copy-done.3 = f32[1,1,8,1024]{3,2,1,0:T(8,128)S(1)} copy-done((f32[1,1,8,1024]{3,2,1,0:T(8,128)S(1)}, f32[1,1,8,1024]{3,2,1,0:T(8,128)}, u32[]{:S(2)}) %copy-start.3) | copy-done | bytes 32792
  4.1 0.0 copy-start.4
  4.1 0.7 %copy-done.4 = s32[1,2,16]{2,1,0:T(2,128)S(1)} copy-done((s32[1,2,16]{2,1,0:T(2,128)S(1)}, s32[1,2,16]{2,1,0:T(2,128)}, u32[]{:S(2)}) %copy-start.4) | copy-done | bytes 152
  4.8 0.0 copy-start.5
  4.8 0.7 %copy-done.5 = s32[1,16]{1,0:T(1,128)S(1)} copy-done((s32[1,16]{1,0:T(1,128)S(1)}, s32[1,16]{1,0:T(1,128)}, u32[]{:S(2)}) %copy-start.5) | copy-done | bytes 88
  5.4 0.0 copy-start.6
  5.4 0.7 %copy-done.6 = f32[16]{0:T(128)S(1)} copy-done((f32[16]{0:T(128)S(1)}, f32[16]{0:T(128)}, u32[]{:S(2)}) %copy-start.6) | copy-done | bytes 88
  6.1 48.2 %shard_map.73 = f32[400,1024]{1,0:T(8,128)S(1)} custom-call(f32[400,1024]{1,0:T(8,128)S(1)} %bitcast.13, bf16[400,1024]{1,0:T(8,128)(2,1)S(1)} %bitcast.14, s32[8,1024]{1,0:T(8,128)S(1)} %bitcast.15, f32[8,1024]{1,0:T(8,128)S(1)} %bitcast.16, s32[1,16]{1,0:T(1,128)S(1)} %copy-done.5, s32[1,2,16]{2,1,0:T(2,128)S(1)} %copy-done.4, f32[16]{0:T(128)S(1)} %copy-done.6), custom_call_target="tpu_custom_call" | custom-call | tf_op jit(solution)/shard_map/pallas_call | solution.py:390
  54.3 1.4 %subtract_bitcast_fusion = f32[1,1024,400]{1,2,0:T(8,128)} fusion(f32[400,1024]{1,0:T(8,128)S(1)} %shard_map.73, f32[1,1024,400]{1,2,0:T(8,128)S(1)} %copy-done), kind=kLoop, calls=%fused_computation | loop fusion | flops 409600 | bytes 4915200 | tf_op jit(solution)/shard_map/broadcast_in_dim | solution.py:400
Async XLA Ops:
  0.0 1.4 %copy-start = (f32[1,1024,400]{1,2,0:T(8,128)S(1)}, f32[1,1024,400]{1,2,0:T(8,128)}, u32[]{:S(2)}) copy-start(f32[1,1024,400]{1,2,0:T(8,128)} %param.7) | copy-start | bytes 4915204
  1.4 1.1 %copy-start.1 = (bf16[1,1024,400]{1,2,0:T(8,128)(2,1)S(1)}, bf16[1,1024,400]{1,2,0:T(8,128)(2,1)}, u32[]{:S(2)}) copy-start(bf16[1,1024,400]{1,2,0:T(8,128)(2,1)} %param.8) | copy-start | bytes 2457604
  2.6 0.8 %copy-start.2 = (s32[1,1,8,1024]{3,2,1,0:T(8,128)S(1)}, s32[1,1,8,1024]{3,2,1,0:T(8,128)}, u32[]{:S(2)}) copy-start(s32[1,1,8,1024]{3,2,1,0:T(8,128)} %param.9) | copy-start | bytes 98308
  3.3 0.8 %copy-start.3 = (f32[1,1,8,1024]{3,2,1,0:T(8,128)S(1)}, f32[1,1,8,1024]{3,2,1,0:T(8,128)}, u32[]{:S(2)}) copy-start(f32[1,1,8,1024]{3,2,1,0:T(8,128)} %param.10) | copy-start | bytes 98308
  4.1 0.7 %copy-start.4 = (s32[1,2,16]{2,1,0:T(2,128)S(1)}, s32[1,2,16]{2,1,0:T(2,128)}, u32[]{:S(2)}) copy-start(s32[1,2,16]{2,1,0:T(2,128)} %shf.1) | copy-start | bytes 388
  4.8 0.7 %copy-start.5 = (s32[1,16]{1,0:T(1,128)S(1)}, s32[1,16]{1,0:T(1,128)}, u32[]{:S(2)}) copy-start(s32[1,16]{1,0:T(1,128)} %cls.1) | copy-start | bytes 196
  5.4 0.7 %copy-start.6 = (f32[16]{0:T(128)S(1)}, f32[16]{0:T(128)}, u32[]{:S(2)}) copy-start(f32[16]{0:T(128)} %dfc.1) | copy-start | bytes 196

commit v5 on v4

--- a/solution.py
+++ b/solution.py
@@ -68,12 +68,13 @@
 
 def kernel(
     n_dom, n_slab, step,
+    vol_hbm, img_hbm, taps_hbm, wts_hbm, cls_hbm, shf_hbm, dfc_hbm,
+    out,
     vol, img, taps, wts, cls, shf, dfc,
-    out,
     mapt, omap, ptap, otap, wide, owide, work, proj, square, back,
     gown, s1send, s1recv, s2send, s2recv, gall, cand, ocand, fs, fx, fy, fz,
     tap_s, tap_r, x_s, x_r, y_s, y_r, z_s, z_r, p_s, p_r, q_s, q_r, g_s, g_r, f_s, f_r, c_s, c_r,
-    ux_s, ux_r, uy_s, uy_r, uz_s, uz_r,
+    ux_s, ux_r, uy_s, uy_r, uz_s, uz_r, in_s,
 ):
     h, d, s = lax.axis_index("half"), lax.axis_index("dom"), lax.axis_index("slab")
     cols, lines = vol.shape
@@ -97,6 +98,16 @@
     for who in everyone:
         pl.semaphore_signal(barrier, inc=1, device_id=who, device_id_type=MESH)
 
+    pairs_in = (
+        (taps_hbm, taps), (wts_hbm, wts), (vol_hbm, vol), (img_hbm, img),
+        (cls_hbm, cls), (shf_hbm, shf), (dfc_hbm, dfc),
+    )
+    inputs = [pltpu.make_async_copy(src, dst, in_s.at[i]) for i, (src, dst) in enumerate(pairs_in)]
+    for copy in inputs:
+        copy.start()
+    inputs[0].wait()
+    inputs[1].wait()
+
     sub = lax.broadcasted_iota(jnp.int32, (8, rows), 0)
     value = jnp.zeros((8, rows), F32)
     block = jnp.zeros((8, rows), F32)
@@ -106,6 +117,8 @@
         value = jnp.where(hit, wts[k:k + 1, :], value)
         block = jnp.where(hit, lax.shift_right_logical(line, 3).astype(F32), block)
     ptap[...] = jnp.concatenate([value, block], axis=0).astype(BF16)
+
+    inputs[2].wait()
 
     @pl.loop(0, lines // CHUNK)
     def _(c):
@@ -139,6 +152,9 @@
             slot = omap.at[p, mine_q * quarter + u]
             y_copies[p][u] = go(remote(slot, slot, y_s.at[p, u], y_r.at[p, u], pair))
             z_copies[p][u] = go(remote(slot, slot, z_s.at[p, u], z_r.at[p, u], zpair))
+
+    for copy in inputs[3:]:
+        copy.wait()
 
     build_matrix(ptap, wide)
     forward(0)
@@ -330,7 +346,7 @@
             pl.when(needed)(copy.wait_recv)
     if bw % CHUNK == 0:
         for b in range(n_dom):
-            out[:, b * bw:(b + 1) * bw] = column * gall[b].astype(F32)
+            out[:, b * bw:(b + 1) * bw] = (column * gall[b].astype(F32)).astype(BF16)
     else:
         fold = CHUNK // bw
 
@@ -339,7 +355,7 @@
             whole = jnp.zeros((cols, CHUNK), F32)
             for u in range(fold):
                 whole = whole + jnp.dot(gall[c * fold + u], placing(bw, u * bw), preferred_element_type=F32)
-            out[:, pl.ds(pl.multiple_of(c * CHUNK, CHUNK), CHUNK)] = column * whole
+            out[:, pl.ds(pl.multiple_of(c * CHUNK, CHUNK), CHUNK)] = (column * whole).astype(BF16)
 
     for copy, needed in sends:
         if needed is None:
@@ -358,8 +374,14 @@
     nc, np_, nq = lines // CHUNK, n_slab - 1, lines // CHUNK // 4
     dma = pltpu.SemaphoreType.DMA
     vmem = pl.BlockSpec(memory_space=pltpu.VMEM)
-    smem = pl.BlockSpec(memory_space=pltpu.SMEM)
     scratch = [
+        pltpu.VMEM((cols, lines), F32),
+        pltpu.VMEM((cols, rows), BF16),
+        pltpu.VMEM(tap_index.shape[2:], jnp.int32),
+        pltpu.VMEM(tap_weight.shape[2:], F32),
+        pltpu.SMEM(classes.shape, jnp.int32),
+        pltpu.SMEM(shifts.shape, jnp.int32),
+        pltpu.SMEM(defocus.shape, F32),
         pltpu.VMEM((nc, cols, CHUNK), BF16),
         pltpu.VMEM((np_, nc, cols, CHUNK), BF16),
         pltpu.VMEM((16, rows), BF16),
@@ -387,17 +409,18 @@
         (np_,), (np_, 2 * nq), (np_, nq), (np_, nq), (nz, 2), (nz - 1, 2), (2, nz - 1, 2), (2, nz, 2), (1,), (np_,), (1,), (nz - 1,)
     ):
         scratch += [dma(shape), dma(shape)]
+    scratch.append(dma((7,)))
     change = pl.pallas_call(
         functools.partial(kernel, n_dom, n_slab, step),
-        out_shape=jax.ShapeDtypeStruct((cols, lines), F32),
-        in_specs=[vmem] * 4 + [smem] * 3,
+        out_shape=jax.ShapeDtypeStruct((cols, lines), BF16),
+        in_specs=[pl.BlockSpec(memory_space=pltpu.HBM)] * 7,
         out_specs=vmem,
         scratch_shapes=scratch,
         compiler_params=pltpu.CompilerParams(
-            collective_id=0, has_side_effects=True, vmem_limit_bytes=30 * 1024 * 1024
+            collective_id=0, has_side_effects=True, vmem_limit_bytes=60 * 1024 * 1024
         ),
     )(slab_map, data, tap_index[0, 0], tap_weight[0, 0], classes, shifts, defocus)
-    return (slab_map - change).T[None]
+    return (slab_map - change.astype(F32)).T[None]
 
 
 def solution(mesh):

time: 56.1 us -> 52.3 us (0.932)
  local copies, waits for them, and re-layouts: 6.08 us -> 0.01 us
  Pallas kernels: 48.2 us -> 49.5 us
  other arithmetic: 1.44 us -> 2.63 us
    unnamed x14 -> x2, local copies, waits for them, and re-layouts: 6.08 us -> 0.01 us
    pallas_call x1, Pallas kernels: 48.2 us -> 49.5 us  [body(): pl.pallas_call(functools.partial(kernel, n_dom, n_slab, step), out_shape=...]
    broadcast_in_dim x1, other arithmetic: 1.44 us -> 2.63 us  [body(): return (slab_map - change.astype(F32)).T[None]]
where the time goes in v5:
time: 52.3 us; the launch traced here: 52.1 us
  Pallas kernels  49.5 us (95%)
  other arithmetic  2.63 us (5%)
    pallas_call x1, Pallas kernels, body(): pl.pallas_call(functools.partial(kernel, n_dom, n_slab, step), out_shape=...  49.5 us
    broadcast_in_dim x1, other arithmetic, body(): return (slab_map - change.astype(F32)).T[None]  2.63 us

profile of v5, /device:TPU:0, one launch (start us, length us, event | category | flops | bytes accessed | tf_op | source)
XLA Modules:
  0.0 52.1 jit_solution(18114323999321229634)
XLA Ops:
  0.0 0.0 copy-start
  0.0 49.5 %shard_map.73 = bf16[400,1024]{1,0:T(8,128)(2,1)} custom-call(f32[400,1024]{1,0:T(8,128)} %bitcast.13, bf16[400,1024]{1,0:T(8,128)(2,1)} %bitcast.14, s32[8,1024]{1,0:T(8,128)} %bitcast.15, f32[8,1024]{1,0:T(8,128)} %bitcast.16, s32[1,16]{1,0:T(1,128)} %cls_hbm.1, s32[1,2,16]{2,1,0:T(2,128)} %shf_hbm.1, f32[16]{0:T(128)} %dfc_hbm.1), custom_call_target="tpu_custom_call" | custom-call | tf_op jit(solution)/shard_map/pallas_call | solution.py:413
  49.5 0.0 copy-done
  49.5 2.6 %subtract_bitcast_fusion = f32[1,1024,400]{1,2,0:T(8,128)} fusion(bf16[400,1024]{1,0:T(8,128)(2,1)} %shard_map.73, f32[1,1024,400]{1,2,0:T(8,128)S(1)} %copy-done), kind=kLoop, calls=%fused_computation | loop fusion | flops 819200 | bytes 4096000 | tf_op jit(solution)/shard_map/broadcast_in_dim | solution.py:423
Async XLA Ops:
  0.0 49.5 %copy-start = (f32[1,1024,400]{1,2,0:T(8,128)S(1)}, f32[1,1024,400]{1,2,0:T(8,128)}, u32[]{:S(2)}) copy-start(f32[1,1024,400]{1,2,0:T(8,128)} %param.7) | copy-start | bytes 4915204

commit v6 on v5

--- a/solution.py
+++ b/solution.py
@@ -286,9 +286,10 @@
                 part = share(source, u)
                 come = remote(part, part, g_s.at[way, k - 1, u], g_r.at[way, k - 1, u], pair)
                 pl.when(needed)(come.wait_recv)
-                from_pair(way, k, u, source, needed)
             if k < nz - 1:
                 relay(k, u)
+            for way, source, needed in ((0, z - k, z - k >= 0), (1, z + k, z + k < nz)):
+                from_pair(way, k, u, source, needed)
 
     if bw % CHUNK == 0:
         mine = vol[:, pl.ds(pl.multiple_of(d * bw, CHUNK), bw)]

time: 52.3 us -> 52.3 us (level)
  no operation moved by 1% of the time
where the time goes in v6:
time: 52.3 us; the launch traced here: 52.1 us
  Pallas kernels  49.5 us (95%)
  other arithmetic  2.63 us (5%)
    pallas_call x1, Pallas kernels, body(): pl.pallas_call(functools.partial(kernel, n_dom, n_slab, step), out_shape=...  49.5 us
    broadcast_in_dim x1, other arithmetic, body(): return (slab_map - change.astype(F32)).T[None]  2.63 us

profile of v6, /device:TPU:0, one launch (start us, length us, event | category | flops | bytes accessed | tf_op | source)
XLA Modules:
  0.0 52.1 jit_solution(11631480406576534226)
XLA Ops:
  0.0 0.0 copy-start
  0.0 49.5 %shard_map.73 = bf16[400,1024]{1,0:T(8,128)(2,1)} custom-call(f32[400,1024]{1,0:T(8,128)} %bitcast.13, bf16[400,1024]{1,0:T(8,128)(2,1)} %bitcast.14, s32[8,1024]{1,0:T(8,128)} %bitcast.15, f32[8,1024]{1,0:T(8,128)} %bitcast.16, s32[1,16]{1,0:T(1,128)} %cls_hbm.1, s32[1,2,16]{2,1,0:T(2,128)} %shf_hbm.1, f32[16]{0:T(128)} %dfc_hbm.1), custom_call_target="tpu_custom_call" | custom-call | tf_op jit(solution)/shard_map/pallas_call | solution.py:414
  49.5 0.0 copy-done
  49.5 2.6 %subtract_bitcast_fusion = f32[1,1024,400]{1,2,0:T(8,128)} fusion(bf16[400,1024]{1,0:T(8,128)(2,1)} %shard_map.73, f32[1,1024,400]{1,2,0:T(8,128)S(1)} %copy-done), kind=kLoop, calls=%fused_computation | loop fusion | flops 819200 | bytes 4096000 | tf_op jit(solution)/shard_map/broadcast_in_dim | solution.py:424
Async XLA Ops:
  0.0 49.5 %copy-start = (f32[1,1024,400]{1,2,0:T(8,128)S(1)}, f32[1,1024,400]{1,2,0:T(8,128)}, u32[]{:S(2)}) copy-start(f32[1,1024,400]{1,2,0:T(8,128)} %param.7) | copy-start | bytes 4915204

commit v7 on v5

--- a/solution.py
+++ b/solution.py
@@ -74,7 +74,7 @@
     mapt, omap, ptap, otap, wide, owide, work, proj, square, back,
     gown, s1send, s1recv, s2send, s2recv, gall, cand, ocand, fs, fx, fy, fz,
     tap_s, tap_r, x_s, x_r, y_s, y_r, z_s, z_r, p_s, p_r, q_s, q_r, g_s, g_r, f_s, f_r, c_s, c_r,
-    ux_s, ux_r, uy_s, uy_r, uz_s, uz_r, in_s,
+    ux_s, ux_r, uy_s, uy_r, uz_s, uz_r, e_s, e_r, in_s,
 ):
     h, d, s = lax.axis_index("half"), lax.axis_index("dom"), lax.axis_index("slab")
     cols, lines = vol.shape
@@ -136,9 +136,14 @@
         return copy
 
     tap_copies = [go(remote(ptap, otap.at[p], tap_s.at[p], tap_r.at[p], peers[p])) for p in range(n_slab - 1)]
+    top, rest = pl.ds(0, cols // 32 * 16), pl.ds(cols // 32 * 16, cols - cols // 32 * 16)
+
+    def held(ref, i):
+        return ref.at[top, :] if i == quarter else ref
+
     x_copies = [
         [
-            go(remote(mapt.at[c], omap.at[p, c], x_s.at[p, i], x_r.at[p, i], peers[p]))
+            go(remote(held(mapt.at[c], i), held(omap.at[p, c], i), x_s.at[p, i], x_r.at[p, i], peers[p]))
             for i, c in enumerate([g * quarter + u for g in (mine_q, diag_q) for u in range(quarter)])
         ]
         for p in range(n_slab - 1)
@@ -203,12 +208,17 @@
         return e_re * turn_re - e_im * turn_im, e_re * turn_im + e_im * turn_re
 
     lax.fori_loop(0, radii // 8, phase_step, (start_re, start_im))
+    extra = []
+    for p in range(n_slab - 1):
+        z_copies[p][0].wait_recv()
+        slot = omap.at[p, z_q * quarter, rest, :]
+        extra.append(go(remote(slot, slot, e_s.at[p], e_r.at[p], pair)))
 
     for p in range(n_slab - 1):
         tap_copies[p].wait_recv()
         build_matrix(otap.at[p], owide)
         for g, copies in (
-            (mine_q, []), (y_q, y_copies[p]), (z_q, z_copies[p]), (diag_q, x_copies[p][quarter:])
+            (mine_q, []), (y_q, y_copies[p]), (z_q, z_copies[p][1:]), (diag_q, x_copies[p][quarter:] + [extra[p]])
         ):
             for copy in copies:
                 copy.wait_recv()
@@ -406,7 +416,7 @@
         pltpu.VMEM((nz - 1, 8, cols // 2), F32),
     ]
     for shape in (
-        (np_,), (np_, 2 * nq), (np_, nq), (np_, nq), (nz, 2), (nz - 1, 2), (2, nz - 1, 2), (2, nz, 2), (1,), (np_,), (1,), (nz - 1,)
+        (np_,), (np_, 2 * nq), (np_, nq), (np_, nq), (nz, 2), (nz - 1, 2), (2, nz - 1, 2), (2, nz, 2), (1,), (np_,), (1,), (nz - 1,), (np_,)
     ):
         scratch += [dma(shape), dma(shape)]
     scratch.append(dma((7,)))

time: 52.3 us -> 52.3 us (level)
  no operation moved by 1% of the time
where the time goes in v7:
time: 52.3 us; the launch traced here: 52.2 us
  Pallas kernels  49.5 us (95%)
  other arithmetic  2.63 us (5%)
    pallas_call x1, Pallas kernels, body(): pl.pallas_call(functools.partial(kernel, n_dom, n_slab, step), out_shape=...  49.5 us
    broadcast_in_dim x1, other arithmetic, body(): return (slab_map - change.astype(F32)).T[None]  2.63 us

profile of v7, /device:TPU:0, one launch (start us, length us, event | category | flops | bytes accessed | tf_op | source)
XLA Modules:
  0.0 52.2 jit_solution(6623963149540852270)
XLA Ops:
  0.0 0.0 copy-start
  0.0 49.5 %shard_map.73 = bf16[400,1024]{1,0:T(8,128)(2,1)} custom-call(f32[400,1024]{1,0:T(8,128)} %bitcast.13, bf16[400,1024]{1,0:T(8,128)(2,1)} %bitcast.14, s32[8,1024]{1,0:T(8,128)} %bitcast.15, f32[8,1024]{1,0:T(8,128)} %bitcast.16, s32[1,16]{1,0:T(1,128)} %cls_hbm.1, s32[1,2,16]{2,1,0:T(2,128)} %shf_hbm.1, f32[16]{0:T(128)} %dfc_hbm.1), custom_call_target="tpu_custom_call" | custom-call | tf_op jit(solution)/shard_map/pallas_call | solution.py:423
  49.5 0.0 copy-done
  49.5 2.6 %subtract_bitcast_fusion = f32[1,1024,400]{1,2,0:T(8,128)} fusion(bf16[400,1024]{1,0:T(8,128)(2,1)} %shard_map.73, f32[1,1024,400]{1,2,0:T(8,128)S(1)} %copy-done), kind=kLoop, calls=%fused_computation | loop fusion | flops 819200 | bytes 4096000 | tf_op jit(solution)/shard_map/broadcast_in_dim | solution.py:433
Async XLA Ops:
  0.0 49.5 %copy-start = (f32[1,1024,400]{1,2,0:T(8,128)S(1)}, f32[1,1024,400]{1,2,0:T(8,128)}, u32[]{:S(2)}) copy-start(f32[1,1024,400]{1,2,0:T(8,128)} %param.7) | copy-start | bytes 4915204
